TPU v7x, 32 devices: a whole 2x2x4 slice. The times are simulated.
32 devices in a mesh: groups: 2 (over y), space: 4 (over x, core), dp: 4 (over z).
Axes of the slice: x: 2, y: 2, z: 4, core: 2. Of those that a mesh axis runs over, the one named last changes fastest.
Arguments:
- inputs: bfloat16 [8, 8, 128, 768], P(('groups', 'dp'), 'space'), parts along dimension 0, may hold values from -6 to 6
- cotangent: bfloat16 [8, 8, 128, 768], P(('groups', 'dp'), 'space'), parts along dimension 0, may hold values from -6 to 6
- kernel_raw: float32 [768, 1152], P('dp'), may hold values from -0.1875 to 0.1875
- kernel_gain: float32 [768], P('dp'), may hold values from 0.25 to 1.75
Outputs:
- grad_inputs: bfloat16 [8, 8, 128, 768], P(('groups', 'dp'), 'space'), parts along dimension 0
- grad_raw: float32 [1536, 1152], P(('groups', 'dp')), parts along dimension 0
- grad_gain: float32 [1536], P(('groups', 'dp')), parts along dimension 0
There are 2 independent parts, one for each index of `groups`. A program takes and returns all parts, laid end to end along the dimension named above; an argument that names none is the same for every part. Nothing has to cross between parts.
All inputs are finite; a program needn't handle non-finite values.
Results may differ from a plain program's by a relative error of at most 0.0052.
Values may be sent and summed in bfloat16 or wider, within the bound.
A program may use at most 64 MiB of HBM per device.

v0:
```python
import math

import jax
import jax.numpy as jnp
from jax import lax
from jax.sharding import PartitionSpec as P

act_gain = 1.7015
alpha_skip = 0.2


def padded_2(value, sides, width):
    for axis, dim in sides:
        size, length = (lax.axis_size(axis), value.shape[dim])
        up = [(i, (i + 1) % size) for i in range(size - 1)]
        down = [(j, i) for i, j in up]
        last = lax.slice_in_dim(value, length - width, length, axis=dim)
        first = lax.slice_in_dim(value, 0, width, axis=dim)
        before = lax.ppermute(last, axis, up)
        after = lax.ppermute(first, axis, down)
        value = jnp.concatenate([before, value, after], axis=dim)
    return value


def activate(value_in):
    return act_gain * jax.nn.gelu(value_in, approximate=False)


def ws_parts(kernel_rows):
    row_mean = jnp.mean(kernel_rows, axis=1, keepdims=True)
    centred = kernel_rows - row_mean
    row_var = jnp.mean(centred * centred, axis=1, keepdims=True)
    inv_std = lax.rsqrt(row_var + 1e-05)
    return (centred * inv_std, inv_std)


def ws_back(grad_standard, unit, inv_std, gains):
    fan_scale = 1.0 / math.sqrt(unit.shape[1])
    grad_gain = jnp.sum(grad_standard * unit, axis=1) * fan_scale
    grad_unit = grad_standard * gains[:, None] * fan_scale
    centre_term = jnp.mean(grad_unit, axis=1, keepdims=True)
    along_term = jnp.mean(grad_unit * unit, axis=1, keepdims=True)
    grad_raw = inv_std * (grad_unit - centre_term - unit * along_term)
    return (grad_raw, grad_gain)


def local(inputs, cotangent, kernel_raw, kernel_gain):
    images, band_rows, band_cols, chan_count = inputs.shape
    fan_size = kernel_raw.shape[1]
    group_width = fan_size // 9
    group_count = chan_count // group_width
    fan_scale = 1.0 / math.sqrt(fan_size)
    inputs_wide = inputs.astype(jnp.float32)
    hidden = activate(inputs_wide).astype(jnp.bfloat16)
    grad_conv = (alpha_skip * cotangent.astype(jnp.float32)).astype(jnp.bfloat16)
    stacked = jnp.stack([hidden, grad_conv])
    rimmed = padded_2(stacked, (("space", 2),), 1)
    padded = jnp.pad(rimmed, ((0, 0), (0, 0), (0, 0), (1, 1), (0, 0)))
    hidden_pad = padded[0]
    grad_pad = padded[1]
    unit, inv_std = ws_parts(kernel_raw)
    standard_rows = (kernel_gain[:, None] * unit * fan_scale).astype(jnp.bfloat16)
    standard = lax.all_gather(standard_rows, "dp", axis=0, tiled=True)
    tap_kernels = standard.reshape(group_count, group_width, 3, 3, group_width)
    count = images * band_rows * band_cols
    grad_flat = grad_conv.reshape(count, group_count, group_width)
    grad_hidden = jnp.zeros((count, group_count, group_width), jnp.float32)
    tap_grads = []
    for tap_row in range(3):
        backed_cols = []
        for tap_col in range(3):
            shifted = hidden_pad[:, tap_row : tap_row + band_rows, tap_col : tap_col + band_cols]
            shifted = shifted.reshape(count, group_count, group_width)
            tap_grads.append(
                jnp.einsum("mgo,mgi->goi", grad_flat, shifted, preferred_element_type=jnp.float32)
            )
            backed = grad_pad[
                :, 2 - tap_row : 2 - tap_row + band_rows, 2 - tap_col : 2 - tap_col + band_cols
            ]
            backed_cols.append(backed.reshape(count, group_count, group_width))
        backed_row = jnp.stack(backed_cols, axis=2)
        grad_hidden = grad_hidden + jnp.einsum(
            "mgbo,gobi->mgi",
            backed_row,
            tap_kernels[:, :, tap_row],
            preferred_element_type=jnp.float32,
        )
    total_images = images * lax.axis_size("dp")
    grad_standard = jnp.stack(tap_grads, axis=2).reshape(chan_count, fan_size) * (
        1.0 / total_images
    )
    unused_act, pull_act = jax.vjp(activate, inputs_wide)
    grad_inputs = cotangent.astype(jnp.float32) + pull_act(grad_hidden.reshape(inputs.shape))[0]
    band_count = lax.axis_size("space")
    data_count = lax.axis_size("dp")
    owner_rows = kernel_raw.shape[0]
    piece_rows = owner_rows // band_count
    ordered = grad_standard.reshape(data_count, band_count, piece_rows, fan_size)
    ordered = ordered.transpose(1, 0, 2, 3).reshape(chan_count, fan_size)
    piece = lax.psum_scatter(ordered, ("space", "dp"), scatter_dimension=0, tiled=True)
    start = lax.axis_index("space") * piece_rows
    unit_piece = lax.dynamic_slice_in_dim(unit, start, piece_rows, 0)
    inv_piece = lax.dynamic_slice_in_dim(inv_std, start, piece_rows, 0)
    gain_piece = lax.dynamic_slice_in_dim(kernel_gain, start, piece_rows, 0)
    raw_piece, gain_grad_piece = ws_back(piece, unit_piece, inv_piece, gain_piece)
    grad_raw, grad_gain = (
        lax.all_gather(raw_piece, "space", axis=0, tiled=True),
        lax.all_gather(gain_grad_piece, "space", axis=0, tiled=True),
    )
    return (grad_inputs.astype(jnp.bfloat16), grad_raw, grad_gain)


def solution(mesh):
    placed = (
        P(("groups", "dp"), "space", None, None),
        P(("groups", "dp"), "space", None, None),
        P("dp", None),
        P("dp"),
    )
    return jax.shard_map(
        local,
        mesh=mesh,
        in_specs=placed,
        out_specs=(
            P(("groups", "dp"), "space", None, None),
            P(("groups", "dp"), None),
            P(("groups", "dp")),
        ),
        check_vma=False,
    )
```

profile of v0, /device:TPU:1, one launch (start us, length us, event | category | flops | bytes accessed | tf_op | source)
XLA Modules:
  0.0 154.4 jit_solution(8007372213218022565)
XLA Ops:
  8.1 3.9 %fusion.41 = (bf16[1,2,128,768]{3,2,1,0:T(8,128)(2,1)S(1)}, bf16[1,1,2,128,768]{4,3,2,1,0:T(8,128)(2,1)S(1)}, bf16[1,1,2,128,768]{4,3,2,1,0:T(8,128)(2,1)S(1)}, f32[1,2,128,768]{3,2,1,0:T(8,128)}) fusion(bf16[1,2,128,768]{3,2,1,0:T(8,128)(2,1)} %param.5, bf16[1,2,128,768]{3,2,1,0:T(8,128)(2,1)} %param.4), kind=kLoop, calls=%fused_computation.68 | loop fusion | flops 13762560 | bytes 2752512 | tf_op jit(solution)/shard_map/convert_element_type | solution.py:55
  11.9 0.8 fusion.74
  12.7 2.0 %collective-permute-start.1 = (bf16[2,1,1,128,768]{4,3,2,1,0:T(8,128)(2,1)}, bf16[2,1,1,128,768]{4,3,2,1,0:T(8,128)(2,1)S(1)}, u32[]{:S(2)}, u32[]{:S(2)}) collective-permute-start(bf16[2,1,1,128,768]{4,3,2,1,0:T(8,128)(2,1)} %get-tuple-element.34), channel_id=1, source_target_pairs={{4,0},{8,4},{12,8},{5,1},{9,5},{13,9},{6,2},{10,6},{14,10},{7,3},{... | collective-permute-start | bytes 1179656 | tf_op jit(solution)/shard_map/ppermute | solution.py:20
  14.7 4.5 %collective-permute-start = (bf16[2,1,1,128,768]{4,3,2,1,0:T(8,128)(2,1)S(1)}, bf16[2,1,1,128,768]{4,3,2,1,0:T(8,128)(2,1)S(1)}, u32[]{:S(2)}, u32[]{:S(2)}) collective-permute-start(bf16[2,1,1,128,768]{4,3,2,1,0:T(8,128)(2,1)S(1)} %get-tuple-element.33), channel_id=1, source_target_pairs={{0,4},{4,8},{8,12},{1,5},{5,9},{9,13},{2,6},{6,10},{10,14},{3,7},{... | collective-permute-start | bytes 1179656 | tf_op jit(solution)/shard_map/ppermute | solution.py:19
  19.6 1.3 multiply_convert_fusion
  21.9 1.1 collective-permute-done.1
  22.9 1.0 collective-permute-done
  24.4 1.5 fusion.92
  25.9 2.2 %reshape.128 = bf16[256,6,128]{2,1,0:T(8,128)(2,1)} reshape(bf16[1,2,128,768]{3,2,1,0:T(8,128)(2,1)} %get-tuple-element.23) | data formatting | bytes 786432 | tf_op jit(solution)/shard_map/reshape | solution.py:73
  28.2 2.3 %reshape.129 = bf16[256,6,128]{2,1,0:T(8,128)(2,1)} reshape(bf16[1,2,128,768]{3,2,1,0:T(8,128)(2,1)} %get-tuple-element.22) | data formatting | bytes 786432 | tf_op jit(solution)/shard_map/reshape | solution.py:73
  30.4 2.3 %reshape.130 = bf16[256,6,128]{2,1,0:T(8,128)(2,1)} reshape(bf16[1,2,128,768]{3,2,1,0:T(8,128)(2,1)} %get-tuple-element.21) | data formatting | bytes 786432 | tf_op jit(solution)/shard_map/reshape | solution.py:73
  32.7 1.3 reshape.131
  34.0 1.3 reshape.132
  36.6 1.5 reshape.136
  38.1 1.4 fusion.16
  39.5 1.3 fusion.15
  40.8 1.3 fusion.14
  43.9 4.9 %copy.105 = f32[6,128,9,128]{3,2,1,0:T(8,128)} copy(f32[6,128,9,128]{3,1,0,2:T(8,128)S(1)} %broadcast_multiply_fusion) | data formatting | bytes 7077888 | tf_op jit(solution)/shard_map/mul | solution.py:89
  48.8 6.2 %mul.165 = f32[4,4,48,1152]{3,2,1,0:T(8,128)} reshape(f32[6,128,9,128]{3,2,1,0:T(8,128)} %copy.105) | data formatting | bytes 7077888 | tf_op jit(solution)/shard_map/mul | solution.py:89
  55.0 4.0 %copy.106 = f32[4,4,48,1152]{3,2,1,0:T(8,128)} copy(f32[4,4,48,1152]{3,2,0,1:T(8,128)} %bitcast.125) | data formatting | bytes 7077888 | tf_op jit(solution)/shard_map/transpose | solution.py:99
  59.6 0.6 dynamic-slice.4
  60.9 1.4 fusion.93
  62.3 1.4 reshape.127
  63.7 0.8 copy.83
  64.5 1.4 reshape.126
  66.0 0.8 copy.82
  66.8 1.5 reshape.125
  68.3 0.8 copy.81
  69.5 0.8 copy.76
  70.8 0.8 copy.75
  72.1 0.8 copy.74
  73.3 0.8 copy.69
  74.6 0.8 copy.68
  75.8 0.8 copy.67
  76.7 3.3 %reshape.137 = bf16[6,128,3,3,128]{4,3,2,1,0:T(4,128)(2,1)S(1)} reshape(bf16[768,1152]{1,0:T(8,128)(2,1)} %all-gather.2.cloned.1.call-done) | data formatting | bytes 3538944 | tf_op jit(solution)/shard_map/reshape | solution.py:64
  80.0 2.3 %fusion.91 = (bf16[6,128,1,3,128]{4,3,2,1,0:T(4,128)(2,1)S(1)}, bf16[6,128,1,3,128]{4,3,2,1,0:T(4,128)(2,1)}, bf16[6,128,1,3,128]{4,3,2,1,0:T(4,128)(2,1)}) fusion(bf16[6,128,3,3,128]{4,3,2,1,0:T(4,128)(2,1)S(1)} %reshape.137), kind=kLoop, calls=%fused_computation.129 | loop fusion | bytes 3538944 | tf_op jit(solution)/shard_map/slice | solution.py:85
  82.3 1.5 copy.168
  83.9 1.5 copy.167
  85.3 0.5 copy.166
  85.9 1.7 %convolution_bitcast_fusion = f32[6,128,256]{2,1,0:T(8,128)S(1)} fusion(bf16[256,6,1,128]{3,0,2,1:T(8,128)(2,1)S(1)} %copy-done.5, bf16[256,6,1,128]{3,0,2,1:T(8,128)(2,1)S(1)} %copy-done.6, bf16[256,6,1,128]{3,0,2,1:T(8,128)(2,1)} %copy.81, bf16[6,128,1,3,128]{1,4,3,0,2:T(8,128)(2,1)S(1)} %copy.168), kind=kOutput, calls=%fused_computation.9 | convolution fusion | flops 152174592 | bytes 2555904 | tf_op jit(solution)/shard_map/mgbo,gobi->mgi/dot_general | solution.py:82
  88.2 0.5 fusion.7
  89.6 2.5 %fusion.42 = bf16[1,2,128,768]{3,2,1,0:T(8,128)(2,1)} fusion(f32[1,2,128,768]{3,2,1,0:T(8,128)S(1)} %copy.84, bf16[1,2,128,768]{3,2,1,0:T(8,128)(2,1)} %param.4, bf16[1,2,128,768]{3,2,1,0:T(8,128)(2,1)} %param.5, f32[1,2,128,768]{3,2,1,0:T(8,128)S(1)} %copy-done.1), kind=kLoop, calls=%fused_computation.69 | loop fusion | flops 3342336 | bytes 2752512 | tf_op jit(solution)/shard_map/convert_element_type | solution.py:110
  92.1 35.6 %reduce-scatter.2.cloned.1.call-done = f32[48,1152]{1,0:T(8,128)} async-done(((f32[768,1152]{1,0:T(8,128)}), f32[48,1152]{1,0:T(8,128)}) %reduce-scatter.2.cloned.1.call-update) | async-done | bytes 221200 | tf_op jit(solution)/shard_map/reduce_scatter | solution.py:100
  127.7 1.2 multiply_reduce_fusion.1
  128.9 1.1 subtract_multiply_fusion.1
  129.9 10.3 %all_gather.10 = f32[192,1152]{1,0:T(8,128)S(1)} all-gather(f32[48,1152]{1,0:T(8,128)S(1)} %subtract_multiply_fusion.1), channel_id=1, replica_groups=mesh['groups'=2,'space'=4,'dp'=4] {'space'}, dimensions={0}, use_global_device_ids=true | all-gather | bytes 1105920 | tf_op jit(solution)/shard_map/all_gather | solution.py:107
  140.4 5.7 %all-reduce.1 = f32[192]{0:T(256)} all-reduce(f32[192]{0:T(256)S(1)} %multiply_dynamic-update-slice_fusion), channel_id=1, replica_groups=mesh['groups'=2,'space'=4,'dp'=4] {'space'}, use_global_device_ids=true, to_apply=%add.1 | all-reduce | flops 192 | bytes 1536
  146.1 0.9 copy.197
  (68 shorter events, 9.9 us)
Async XLA Ops:
  8.0 11.2 %copy-start = (f32[192,1152]{1,0:T(8,128)S(1)}, f32[192,1152]{1,0:T(8,128)}, u32[]{:S(2)}) copy-start(f32[192,1152]{1,0:T(8,128)} %param.6) | copy-start | bytes 2654212
  8.0 11.6 %copy-start.13 = (f32[192]{0:T(256)S(1)}, f32[192]{0:T(256)}, u32[]{:S(2)}) copy-start(f32[192]{0:T(256)} %param.7) | copy-start | bytes 2308
  8.0 68.7 %all-gather.2.cloned.1.call-start = ((), (), s32[]{:S(2)}) async-start(), calls=%async_computation.1 | async-start | bytes 2211840 | tf_op jit(solution)/shard_map/all_gather | solution.py:63
  12.7 10.2 %collective-permute-start.1 = (bf16[2,1,1,128,768]{4,3,2,1,0:T(8,128)(2,1)}, bf16[2,1,1,128,768]{4,3,2,1,0:T(8,128)(2,1)S(1)}, u32[]{:S(2)}, u32[]{:S(2)}) collective-permute-start(bf16[2,1,1,128,768]{4,3,2,1,0:T(8,128)(2,1)} %get-tuple-element.34), channel_id=1, source_target_pairs={{4,0},{8,4},{12,8},{5,1},{9,5},{13,9},{6,2},{10,6},{14,10},{7,3},{... | collective-permute-start | bytes 1179656 | tf_op jit(solution)/shard_map/ppermute | solution.py:20
  14.7 9.2 %collective-permute-start = (bf16[2,1,1,128,768]{4,3,2,1,0:T(8,128)(2,1)S(1)}, bf16[2,1,1,128,768]{4,3,2,1,0:T(8,128)(2,1)S(1)}, u32[]{:S(2)}, u32[]{:S(2)}) collective-permute-start(bf16[2,1,1,128,768]{4,3,2,1,0:T(8,128)(2,1)S(1)} %get-tuple-element.33), channel_id=1, source_target_pairs={{0,4},{4,8},{8,12},{1,5},{5,9},{9,13},{2,6},{6,10},{10,14},{3,7},{... | collective-permute-start | bytes 1179656 | tf_op jit(solution)/shard_map/ppermute | solution.py:19
  20.9 106.8 %reduce-scatter.2.cloned.1.call-start = ((), (), s32[]{:S(2)}) async-start(), calls=%async_computation.2 | async-start | bytes 3760128 | tf_op jit(solution)/shard_map/reduce_scatter | solution.py:100
  38.1 4.0 %copy-start.4 = (bf16[256,6,128]{2,1,0:T(8,128)(2,1)S(1)}, bf16[256,6,128]{2,1,0:T(8,128)(2,1)}, u32[]{:S(2)}) copy-start(bf16[256,6,128]{2,1,0:T(8,128)(2,1)} %reshape.131) | copy-start | bytes 1179652
  38.1 4.3 %copy-start.3 = (bf16[256,6,128]{2,1,0:T(8,128)(2,1)S(1)}, bf16[256,6,128]{2,1,0:T(8,128)(2,1)}, u32[]{:S(2)}) copy-start(bf16[256,6,128]{2,1,0:T(8,128)(2,1)} %reshape.132) | copy-start | bytes 1179652
  59.0 0.7 copy-start.14
  80.0 5.8 %copy-start.5 = (bf16[256,6,1,128]{3,0,2,1:T(8,128)(2,1)S(1)}, bf16[256,6,1,128]{3,0,2,1:T(8,128)(2,1)}, u32[]{:S(2)}) copy-start(bf16[256,6,1,128]{3,0,2,1:T(8,128)(2,1)} %copy.83) | copy-start | bytes 1179652
  82.3 3.5 %copy-start.6 = (bf16[256,6,1,128]{3,0,2,1:T(8,128)(2,1)S(1)}, bf16[256,6,1,128]{3,0,2,1:T(8,128)(2,1)}, u32[]{:S(2)}) copy-start(bf16[256,6,1,128]{3,0,2,1:T(8,128)(2,1)} %copy.82) | copy-start | bytes 1179652
  85.9 1.7 %copy-start.7 = (bf16[256,6,1,128]{3,0,2,1:T(8,128)(2,1)S(1)}, bf16[256,6,1,128]{3,0,2,1:T(8,128)(2,1)}, u32[]{:S(2)}) copy-start(bf16[256,6,1,128]{3,0,2,1:T(8,128)(2,1)} %copy.76) | copy-start | bytes 1179652
  85.9 1.7 %copy-start.8 = (bf16[256,6,1,128]{3,0,2,1:T(8,128)(2,1)S(1)}, bf16[256,6,1,128]{3,0,2,1:T(8,128)(2,1)}, u32[]{:S(2)}) copy-start(bf16[256,6,1,128]{3,0,2,1:T(8,128)(2,1)} %copy.75) | copy-start | bytes 1179652
  85.9 1.7 %copy-start.9 = (bf16[256,6,1,128]{3,0,2,1:T(8,128)(2,1)S(1)}, bf16[256,6,1,128]{3,0,2,1:T(8,128)(2,1)}, u32[]{:S(2)}) copy-start(bf16[256,6,1,128]{3,0,2,1:T(8,128)(2,1)} %copy.74) | copy-start | bytes 1179652
  85.9 2.2 %copy-start.10 = (bf16[256,6,1,128]{3,0,2,1:T(8,128)(2,1)S(1)}, bf16[256,6,1,128]{3,0,2,1:T(8,128)(2,1)}, u32[]{:S(2)}) copy-start(bf16[256,6,1,128]{3,0,2,1:T(8,128)(2,1)} %copy.69) | copy-start | bytes 1179652
  85.9 2.2 %copy-start.11 = (bf16[256,6,1,128]{3,0,2,1:T(8,128)(2,1)S(1)}, bf16[256,6,1,128]{3,0,2,1:T(8,128)(2,1)}, u32[]{:S(2)}) copy-start(bf16[256,6,1,128]{3,0,2,1:T(8,128)(2,1)} %copy.68) | copy-start | bytes 1179652
  85.9 2.2 %copy-start.12 = (bf16[256,6,1,128]{3,0,2,1:T(8,128)(2,1)S(1)}, bf16[256,6,1,128]{3,0,2,1:T(8,128)(2,1)}, u32[]{:S(2)}) copy-start(bf16[256,6,1,128]{3,0,2,1:T(8,128)(2,1)} %copy.67) | copy-start | bytes 1179652
  88.2 1.4 copy-start.1
  88.7 38.9 %copy-start.2 = (f32[192,1152]{1,0:T(8,128)S(1)}, f32[192,1152]{1,0:T(8,128)}, u32[]{:S(2)}) copy-start(f32[192,1152]{1,0:T(8,128)} %get-tuple-element.7) | copy-start | bytes 2654212
Sparse Core Ops, SparseCore 0:
  21.0 40.3 all-gather.1
Sparse Core Ops, SparseCore 1:
  59.1 68.5 reduce-scatter.1
where the time goes:
time: 157 us; the launch traced here: 154 us
  local copies, waits for them, and re-layouts  57.4 us (37%)
  waiting for transfers between devices  37.6 us (24%)
  between operations  16.6 us (11%)
  blocking collectives  16 us (10%)
  other arithmetic  11.9 us (8%)
  matrix products  8.19 us (5%)
  starting transfers between devices  6.68 us (4%)
    reduce_scatter x1, waiting for transfers between devices, local(): lax.psum_scatter(ordered, ('space', 'dp'), scatter_dimension=0, tiled=True)  35.6 us
    another operation x18, local copies, waits for them, and re-layouts, local(): backed_row = jnp.stack(backed_cols, axis=2)  14.4 us
    reshape x9, local copies, waits for them, and re-layouts, local(): shifted = shifted.reshape(count, group_count, group_width)  12.1 us
    mul x2, local copies, waits for them, and re-layouts, local(): jnp.stack(tap_grads, axis=2).reshape(chan_count, fan_size)  11.1 us
    all_gather x1, blocking collectives, local(): lax.all_gather(raw_piece, 'space', axis=0, tiled=True)  10.3 us
    unnamed x1, blocking collectives  5.7 us
    unnamed x36, local copies, waits for them, and re-layouts  5.53 us
    dot_general x9, matrix products, local(): jnp.einsum('mgo,mgi->goi', grad_flat, shifted, preferred_element_type=jnp...  5.48 us
  transfers between devices with their start and end apart: 4, of which 3 were waited for; matrix products, arithmetic and copies ran while one was open for 45% of the time, Pallas kernels for 0%

commit v1 on v0

--- a/solution.py
+++ b/solution.py
@@ -1,8 +1,11 @@
+import functools
 import math
 
 import jax
 import jax.numpy as jnp
 from jax import lax
+from jax.experimental import pallas as pl
+from jax.experimental.pallas import tpu as pltpu
 from jax.sharding import PartitionSpec as P
 
 act_gain = 1.7015
@@ -110,6 +113,318 @@
     return (grad_inputs.astype(jnp.bfloat16), grad_raw, grad_gain)
 
 
+MESH = pl.DeviceIdType.MESH
+F32 = jnp.float32
+BF16 = jnp.bfloat16
+
+
+def rows_at(start, size):
+    return pl.ds(pl.multiple_of(start, 16), size)
+
+
+def block_kernel(
+    total_images, data_count,
+    x_ref, cot_ref, raw_ref, gain_ref, grad_ref, ws_ref,
+    halo, gpad, hs, slope, std, part, sendb, got_core, got_x, got_z, gathered,
+    halo_s, halo_r, wz_s, wz_r, wx_s, wx_r, wc_s, wc_r,
+    rc_s, rc_r, rx_s, rx_r, rz_s, rz_r, ag_s, ag_r,
+):
+    pixels, chan_count = x_ref.shape
+    owner_rows, fan_size = raw_ref.shape
+    width = fan_size // 9
+    wide = 3 * width
+    group_count = chan_count // width
+    cols = gpad.shape[0] - pixels
+    cols = cols // 2
+    piece_rows = owner_rows // 4
+    fan_scale = 1.0 / math.sqrt(fan_size)
+    band = lax.axis_index("space")
+    mine = lax.axis_index("dp")
+    core = band % 2
+    pair = band + 1 - 2 * core
+    cross = (band + 2) % 4
+
+    def copy(src, dst, send, recv, where):
+        return pltpu.make_async_remote_copy(
+            src_ref=src, dst_ref=dst, send_sem=send, recv_sem=recv,
+            device_id=where, device_id_type=MESH,
+        )
+
+    barrier = pltpu.get_barrier_semaphore()
+    for j in range(1, 4):
+        pl.semaphore_signal(
+            barrier, inc=1, device_id={"space": (band + j) % 4}, device_id_type=MESH
+        )
+    for j in range(1, data_count):
+        pl.semaphore_signal(
+            barrier, inc=1, device_id={"dp": (mine + j) % data_count}, device_id_type=MESH
+        )
+
+    def unit_of(rows, gains):
+        row_mean = jnp.mean(rows, axis=1, keepdims=True)
+        centred = rows - row_mean
+        row_var = jnp.mean(centred * centred, axis=1, keepdims=True)
+        inv_std = lax.rsqrt(row_var + 1e-05)
+        return centred * inv_std, inv_std
+
+    def std_step(k, carry):
+        rows = rows_at(k * piece_rows, piece_rows)
+        gains = gain_ref[rows, :]
+        unit, _ = unit_of(raw_ref[rows, :], gains)
+        std[rows_at(mine * owner_rows + k * piece_rows, piece_rows), :] = (
+            gains * unit * fan_scale
+        ).astype(BF16)
+        return carry
+
+    lax.fori_loop(0, 4, std_step, 0)
+
+    pl.semaphore_wait(barrier, 2 + data_count)
+
+    up = copy(cot_ref.at[pl.ds(0, cols), :], halo.at[1], halo_s.at[0], halo_r.at[1],
+              {"space": (band + 3) % 4})
+    down = copy(cot_ref.at[pl.ds(pixels - cols, cols), :], halo.at[0], halo_s.at[1], halo_r.at[0],
+                {"space": (band + 1) % 4})
+
+    @pl.when(band > 0)
+    def _():
+        up.start()
+
+    @pl.when(band < 3)
+    def _():
+        down.start()
+
+    def std_piece(owner, quarter):
+        return std.at[rows_at(owner * owner_rows + quarter * piece_rows, piece_rows), :]
+
+    wz = []
+    for j in range(1, data_count):
+        own = std_piece(mine, band)
+        wz.append(copy(own, own, wz_s.at[j - 1], wz_r.at[j - 1],
+                       {"dp": (mine + j) % data_count}))
+        wz[-1].start()
+
+    gpad[pl.ds(cols, pixels), :] = (alpha_skip * cot_ref[...].astype(F32)).astype(BF16)
+
+    row_id = lax.broadcasted_iota(jnp.int32, (pixels, width), 0) % cols
+
+    def act_step(g, carry):
+        at = pl.ds(pl.multiple_of(g * width, width), width)
+        x = x_ref[:, at].astype(F32)
+        cdf = 0.5 * (1.0 + lax.erf(x * math.sqrt(0.5)))
+        hidden = act_gain * (x * cdf)
+        slope[:, at] = act_gain * (cdf + x * (jnp.exp(-0.5 * x * x) * (1.0 / math.sqrt(2.0 * math.pi))))
+        before = jnp.where(row_id == 0, 0.0, pltpu.roll(hidden, 1, 0))
+        after = jnp.where(row_id == cols - 1, 0.0, pltpu.roll(hidden, pixels - 1, 0))
+        for b, value in enumerate((before, hidden, after)):
+            hs[:, pl.ds(pl.multiple_of(g * wide + b * width, width), width)] = value.astype(BF16)
+        return carry
+
+    lax.fori_loop(0, group_count, act_step, 0)
+
+    @pl.when(band > 0)
+    def _():
+        down.wait_recv()
+        gpad[pl.ds(0, cols), :] = (alpha_skip * halo[0].astype(F32)).astype(BF16)
+
+    @pl.when(band == 0)
+    def _():
+        gpad[pl.ds(0, cols), :] = jnp.zeros((cols, chan_count), BF16)
+
+    @pl.when(band < 3)
+    def _():
+        up.wait_recv()
+        gpad[pl.ds(cols + pixels, cols), :] = (alpha_skip * halo[1].astype(F32)).astype(BF16)
+
+    @pl.when(band == 3)
+    def _():
+        gpad[pl.ds(cols + pixels, cols), :] = jnp.zeros((cols, chan_count), BF16)
+
+    def weight_step(g, carry):
+        at = pl.ds(pl.multiple_of(g * width, width), width)
+        right = hs[:, pl.ds(pl.multiple_of(g * wide, width), wide)]
+        for a in range(3):
+            left = gpad[pl.ds((2 - a) * cols, pixels), at]
+            part[pl.ds(pl.multiple_of(g * width, width), width), pl.ds(a * wide, wide)] = (
+                lax.dot_general(left, right, (((0,), (0,)), ((), ())), preferred_element_type=F32)
+            )
+        return carry
+
+    def place(owner, quarter):
+        return rows_at(owner * owner_rows + quarter * piece_rows, piece_rows)
+
+    halves = 2 if data_count % 2 == 0 and group_count % 2 == 0 else 1
+    rc = {}
+    for half in range(halves):
+        lax.fori_loop(
+            half * group_count // halves, (half + 1) * group_count // halves, weight_step, 0
+        )
+        for d in range(half * data_count // halves, (half + 1) * data_count // halves):
+            for t in range(2):
+                at = place(d, 1 - core + 2 * t)
+                sendb[at, :] = part[at, :].astype(BF16)
+                n = 2 * d + t
+                rc[n] = copy(sendb.at[at, :], got_core.at[n], rc_s.at[n], rc_r.at[n],
+                             {"space": pair})
+                rc[n].start()
+
+    rx = []
+    for d in range(data_count):
+        for t in range(2):
+            n = 2 * d + t
+            rc[n].wait_recv()
+        other = cross // 2
+        at = place(d, cross)
+        sendb[at, :] = (part[at, :] + got_core[2 * d + other].astype(F32)).astype(BF16)
+        rx.append(copy(sendb.at[at, :], got_x.at[d], rx_s.at[d], rx_r.at[d], {"space": cross}))
+        rx[-1].start()
+
+    wx = []
+    for j in range(1, data_count):
+        wz[j - 1].wait_recv()
+        piece = std_piece((mine + data_count - j) % data_count, band)
+        wx.append(copy(piece, piece, wx_s.at[j - 1], wx_r.at[j - 1], {"space": cross}))
+        wx[-1].start()
+
+    for d in range(data_count):
+        rx[d].wait_recv()
+        at = place(d, band)
+        total = part[at, :] + got_core[2 * d + band // 2].astype(F32) + got_x[d].astype(F32)
+        part[at, :] = total
+        sendb[at, :] = total.astype(BF16)
+    rz = []
+    for j in range(1, data_count):
+        owner = (mine + j) % data_count
+        rz.append(copy(sendb.at[place(owner, band), :], got_z.at[j - 1], rz_s.at[j - 1],
+                       rz_r.at[j - 1], {"dp": owner}))
+        rz[-1].start()
+
+    wc = []
+    for j in range(1, data_count):
+        wx[j - 1].wait_recv()
+        owner = (mine + data_count - j) % data_count
+        for t, quarter in enumerate((band, cross)):
+            n = 2 * (j - 1) + t
+            piece = std_piece(owner, quarter)
+            wc.append(copy(piece, piece, wc_s.at[n], wc_r.at[n], {"space": pair}))
+            wc[-1].start()
+    for one in wc:
+        one.wait_recv()
+
+    def back_step(g, carry):
+        at = pl.ds(pl.multiple_of(g * width, width), width)
+        left = jnp.concatenate(
+            [gpad[pl.ds((2 - a) * cols, pixels), at] for a in range(3)], axis=1
+        )
+        right = jnp.concatenate([std[at, pl.ds(a * wide, wide)] for a in range(3)], axis=0)
+        y = jnp.dot(left, right, preferred_element_type=F32)
+        low, mid, high = y[:, :width], y[:, width : 2 * width], y[:, 2 * width :]
+        low = jnp.where(row_id == cols - 1, 0.0, pltpu.roll(low, pixels - 1, 0))
+        high = jnp.where(row_id == 0, 0.0, pltpu.roll(high, 1, 0))
+        grad = cot_ref[:, at].astype(F32) + slope[:, at] * (low + mid + high)
+        grad_ref[:, at] = grad.astype(BF16)
+        return carry
+
+    lax.fori_loop(0, group_count // 2, back_step, 0)
+
+    total = part[place(mine, band), :]
+    for j in range(1, data_count):
+        rz[j - 1].wait_recv()
+        total = total + got_z[j - 1].astype(F32)
+    grad_standard = total * (1.0 / total_images)
+    rows = rows_at(band * piece_rows, piece_rows)
+    gains = gain_ref[rows, :]
+    unit, inv_std = unit_of(raw_ref[rows, :], gains)
+    grad_gain = jnp.sum(grad_standard * unit, axis=1, keepdims=True) * fan_scale
+    grad_unit = grad_standard * gains * fan_scale
+    centre_term = jnp.mean(grad_unit, axis=1, keepdims=True)
+    along_term = jnp.mean(grad_unit * unit, axis=1, keepdims=True)
+    grad_raw = inv_std * (grad_unit - centre_term - unit * along_term)
+    high = grad_gain.astype(BF16).astype(F32)
+    low = grad_gain - high
+    lane = lax.broadcasted_iota(jnp.int32, (piece_rows, 128), 1)
+    gathered[band, :, pl.ds(0, fan_size)] = grad_raw.astype(BF16)
+    gathered[band, :, pl.ds(fan_size, 128)] = jnp.where(lane == 0, high, low).astype(BF16)
+    ag = []
+    for j in range(1, 4):
+        ag.append(copy(gathered.at[band], gathered.at[band], ag_s.at[j - 1], ag_r.at[j - 1],
+                       {"space": (band + j) % 4}))
+        ag[-1].start()
+    lax.fori_loop(group_count // 2, group_count, back_step, 0)
+    for one in ag:
+        one.wait_recv()
+    for q in range(4):
+        ws_ref[pl.ds(q * piece_rows, piece_rows), :] = gathered[q]
+
+    @pl.when(band > 0)
+    def _():
+        up.wait_send()
+
+    @pl.when(band < 3)
+    def _():
+        down.wait_send()
+
+    for one in wz + list(rc.values()) + rx + wx + rz + wc + ag:
+        one.wait_send()
+
+
+def local_kernel(inputs, cotangent, kernel_raw, kernel_gain):
+    images, band_rows, band_cols, chan_count = inputs.shape
+    owner_rows, fan_size = kernel_raw.shape
+    data_count = lax.axis_size("dp")
+    pixels = band_rows * band_cols
+    piece_rows = owner_rows // 4
+    width = fan_size // 9
+    dma = pltpu.SemaphoreType.DMA
+    peers = data_count - 1
+    vmem = pl.BlockSpec(memory_space=pltpu.VMEM)
+    grad, packed = pl.pallas_call(
+        functools.partial(block_kernel, images * data_count, data_count),
+        out_shape=(
+            jax.ShapeDtypeStruct((pixels, chan_count), BF16),
+            jax.ShapeDtypeStruct((owner_rows, fan_size + 128), BF16),
+        ),
+        in_specs=[vmem] * 4,
+        out_specs=(vmem, vmem),
+        scratch_shapes=[
+            pltpu.VMEM((2, band_cols, chan_count), BF16),
+            pltpu.VMEM((pixels + 2 * band_cols, chan_count), BF16),
+            pltpu.VMEM((pixels, 3 * chan_count), BF16),
+            pltpu.VMEM((pixels, chan_count), F32),
+            pltpu.VMEM((chan_count, fan_size), BF16),
+            pltpu.VMEM((chan_count, fan_size), F32),
+            pltpu.VMEM((chan_count, fan_size), BF16),
+            pltpu.VMEM((2 * data_count, piece_rows, fan_size), BF16),
+            pltpu.VMEM((data_count, piece_rows, fan_size), BF16),
+            pltpu.VMEM((peers, piece_rows, fan_size), BF16),
+            pltpu.VMEM((4, piece_rows, fan_size + 128), BF16),
+            dma((2,)), dma((2,)),
+            dma((peers,)), dma((peers,)),
+            dma((peers,)), dma((peers,)),
+            dma((2 * peers,)), dma((2 * peers,)),
+            dma((2 * data_count,)), dma((2 * data_count,)),
+            dma((data_count,)), dma((data_count,)),
+            dma((peers,)), dma((peers,)),
+            dma((3,)), dma((3,)),
+        ],
+        compiler_params=pltpu.CompilerParams(
+            collective_id=0, has_side_effects=True, vmem_limit_bytes=48 * 1024 * 1024
+        ),
+        cost_estimate=pl.CostEstimate(
+            flops=4 * pixels * chan_count * fan_size,
+            bytes_accessed=8 * pixels * chan_count,
+            transcendentals=2 * pixels * chan_count,
+        ),
+    )(
+        inputs.reshape(pixels, chan_count),
+        cotangent.reshape(pixels, chan_count),
+        kernel_raw,
+        kernel_gain[:, None],
+    )
+    grad_raw = packed[:, :fan_size].astype(F32)
+    grad_gain = packed[:, fan_size].astype(F32) + packed[:, fan_size + 1].astype(F32)
+    return (grad.reshape(inputs.shape), grad_raw, grad_gain)
+
+
 def solution(mesh):
     placed = (
         P(("groups", "dp"), "space", None, None),
@@ -117,14 +432,31 @@
         P("dp", None),
         P("dp"),
     )
-    return jax.shard_map(
-        local,
-        mesh=mesh,
-        in_specs=placed,
-        out_specs=(
-            P(("groups", "dp"), "space", None, None),
-            P(("groups", "dp"), None),
-            P(("groups", "dp")),
-        ),
-        check_vma=False,
-    )
+
+    def run(inputs, cotangent, kernel_raw, kernel_gain):
+        images, rows, cols, chan_count = inputs.shape
+        fan_size = kernel_raw.shape[1]
+        data_count = mesh.shape["dp"]
+        replicas = mesh.shape["groups"] * data_count
+        fits = (
+            mesh.shape["space"] == 4
+            and images == replicas
+            and chan_count % (64 * data_count) == 0
+            and (chan_count // (fan_size // 9)) % 2 == 0
+            and fan_size % (9 * 128) == 0
+            and cols % 16 == 0
+            and rows % 4 == 0
+        )
+        return jax.shard_map(
+            local_kernel if fits else local,
+            mesh=mesh,
+            in_specs=placed,
+            out_specs=(
+                P(("groups", "dp"), "space", None, None),
+                P(("groups", "dp"), None),
+                P(("groups", "dp")),
+            ),
+            check_vma=False,
+        )(inputs, cotangent, kernel_raw, kernel_gain)
+
+    return run

time: 157 us -> 47.7 us (0.30); the launches traced: 154 us -> 47.5 us
  local copies, waits for them, and re-layouts: 57.4 us -> 4.69 us
  Pallas kernels: 0 us -> 40.4 us
  waiting for transfers between devices: 37.6 us -> 0 us
  blocking collectives: 16 us -> 0 us
  between operations: 16.6 us -> 0.67 us
  other arithmetic: 11.9 us -> 1.72 us
  matrix products: 8.19 us -> 0 us
  starting transfers between devices: 6.68 us -> 0 us
    pallas_call x0 -> x1, Pallas kernels: none -> 40.4 us  [local_kernel(): pl.pallas_call(functools.partial(block_kernel, images * data_count, data_...]
    reduce_scatter x1 -> x0, waiting for transfers between devices: 35.6 us -> none  [local(): lax.psum_scatter(ordered, ('space', 'dp'), scatter_dimension=0, tiled=True)]
    reshape x11 -> x0, local copies, waits for them, and re-layouts: 15.7 us -> none  [the longest x9 12.1 us: local(): shifted = shifted.reshape(count, group_count, group_width)]
    another operation x19 -> x0, local copies, waits for them, and re-layouts: 14.4 us -> none  [the longest x18 14.4 us: local(): backed_row = jnp.stack(backed_cols, axis=2)]
    mul x4 -> x0, local copies, waits for them, and re-layouts: 11.9 us -> none  [the longest x2 11.1 us: local(): jnp.stack(tap_grads, axis=2).reshape(chan_count, fan_size)]
    all_gather x1 -> x0, blocking collectives: 10.3 us -> none  [local(): lax.all_gather(raw_piece, 'space', axis=0, tiled=True)]
    dot_general x12 -> x0, matrix products: 8.19 us -> none  [the longest x9 5.48 us: local(): jnp.einsum('mgo,mgi->goi', grad_flat, shifted, preferred_element_type=jnp...]
    convert_element_type x3 -> x1, other arithmetic: 7.68 us -> 0.97 us  [local_kernel(): grad_raw = packed[:, :fan_size].astype(F32)]
  transfers between devices with their start and end apart: 4 -> 0, of which waited for: 3 -> 0; matrix products, arithmetic and copies ran while one was open for 45% -> 0% of each run, Pallas kernels for 0% -> 0%
where the time goes in v1:
time: 47.7 us; the launch traced here: 47.5 us
  Pallas kernels  40.4 us (85%)
  local copies, waits for them, and re-layouts  4.69 us (10%)
  other arithmetic  1.72 us (4%)
  between operations  0.67 us (1%)
    pallas_call x1, Pallas kernels, local_kernel(): pl.pallas_call(functools.partial(block_kernel, images * data_count, data_...  40.4 us
    unnamed x9, local copies, waits for them, and re-layouts  4.57 us
    convert_element_type x1, other arithmetic, local_kernel(): grad_raw = packed[:, :fan_size].astype(F32)  0.97 us

profile of v1, /device:TPU:1, one launch (start us, length us, event | category | flops | bytes accessed | tf_op | source)
XLA Modules:
  0.0 47.5 jit_solution(11208376646129809558)
XLA Ops:
  0.6 0.0 copy-start.3
  0.6 0.7 %copy-done.3 = f32[192]{0:T(256)S(1)} copy-done((f32[192]{0:T(256)S(1)}, f32[192]{0:T(256)}, u32[]{:S(2)}) %copy-start.3) | copy-done | bytes 792
  1.3 0.1 copy.7.gain_ref
  1.4 0.0 copy-start
  1.4 1.2 %copy-done = f32[192,1152]{1,0:T(8,128)S(1)} copy-done((f32[192,1152]{1,0:T(8,128)S(1)}, f32[192,1152]{1,0:T(8,128)}, u32[]{:S(2)}) %copy-start) | copy-done | bytes 884760
  2.6 0.0 copy-start.1
  2.6 1.0 %copy-done.1 = bf16[1,2,128,768]{3,2,1,0:T(8,128)(2,1)S(1)} copy-done((bf16[1,2,128,768]{3,2,1,0:T(8,128)(2,1)S(1)}, bf16[1,2,128,768]{3,2,1,0:T(8,128)(2,1)}, u32[]{:S(2)}) %copy-start.1) | copy-done | bytes 393240
  3.6 0.0 copy-start.2
  3.6 1.0 %copy-done.2 = bf16[1,2,128,768]{3,2,1,0:T(8,128)(2,1)S(1)} copy-done((bf16[1,2,128,768]{3,2,1,0:T(8,128)(2,1)S(1)}, bf16[1,2,128,768]{3,2,1,0:T(8,128)(2,1)}, u32[]{:S(2)}) %copy-start.2) | copy-done | bytes 393240
  4.6 40.4 %shard_map.67 = (bf16[256,768]{1,0:T(8,128)(2,1)S(1)}, bf16[192,1280]{1,0:T(8,128)(2,1)S(1)}) custom-call(bf16[256,768]{1,0:T(8,128)(2,1)S(1)} %bitcast.5, bf16[256,768]{1,0:T(8,128)(2,1)S(1)} %bitcast.6, f32[192,1152]{1,0:T(8,128)S(1)} %copy-done, f32[192,1]{1,0:T(8,128)S(1)} %copy.7.gain_ref), custom_call_target="tpu_custom_call" | custom-call | flops 905969664 | bytes 1572864 | tf_op jit(solution)/shard_map/pallas_call | solution.py:380
  45.0 0.7 %add_reduce_fusion = f32[192]{0:T(256)} fusion(bf16[192,1280]{1,0:T(8,128)(2,1)S(1)} %get-tuple-element.6), kind=kLoop, calls=%fused_computation.1 | loop fusion | flops 576 | bytes 1536 | tf_op jit(solution)/shard_map/add | solution.py:424
  45.8 1.0 %slice_convert_fusion = f32[192,1152]{1,0:T(8,128)} fusion(bf16[192,1280]{1,0:T(8,128)(2,1)S(1)} %get-tuple-element.6), kind=kLoop, calls=%fused_computation | loop fusion | flops 221184 | bytes 1327104 | tf_op jit(solution)/shard_map/convert_element_type | solution.py:423
  46.7 0.7 %copy.9 = bf16[1,2,128,768]{3,2,1,0:T(8,128)(2,1)} copy(bf16[1,2,128,768]{3,2,1,0:T(8,128)(2,1)S(1)} %bitcast.4) | data formatting | bytes 786432
Async XLA Ops:
  0.6 0.7 %copy-start.3 = (f32[192]{0:T(256)S(1)}, f32[192]{0:T(256)}, u32[]{:S(2)}) copy-start(f32[192]{0:T(256)} %param.7) | copy-start | bytes 2308
  1.4 1.2 %copy-start = (f32[192,1152]{1,0:T(8,128)S(1)}, f32[192,1152]{1,0:T(8,128)}, u32[]{:S(2)}) copy-start(f32[192,1152]{1,0:T(8,128)} %raw_ref.1) | copy-start | bytes 2654212
  2.6 1.0 %copy-start.1 = (bf16[1,2,128,768]{3,2,1,0:T(8,128)(2,1)S(1)}, bf16[1,2,128,768]{3,2,1,0:T(8,128)(2,1)}, u32[]{:S(2)}) copy-start(bf16[1,2,128,768]{3,2,1,0:T(8,128)(2,1)} %param.4) | copy-start | bytes 1179652
  3.6 1.0 %copy-start.2 = (bf16[1,2,128,768]{3,2,1,0:T(8,128)(2,1)S(1)}, bf16[1,2,128,768]{3,2,1,0:T(8,128)(2,1)}, u32[]{:S(2)}) copy-start(bf16[1,2,128,768]{3,2,1,0:T(8,128)(2,1)} %param.5) | copy-start | bytes 1179652

commit v2 on v1

--- a/solution.py
+++ b/solution.py
@@ -124,8 +124,8 @@
 
 def block_kernel(
     total_images, data_count,
-    x_ref, cot_ref, raw_ref, gain_ref, grad_ref, ws_ref,
-    halo, gpad, hs, slope, std, part, sendb, got_core, got_x, got_z, gathered,
+    x_hbm, cot_hbm, raw_hbm, gain_hbm, grad_hbm, ws_hbm, gains_ref,
+    x_ref, cot_ref, raw_ref, gain_row, gain_ref, grad_ref, load_s, out_s, halo, gpad, hs, slope, std, part, sendb, got_core, got_x, got_z, gathered,
     halo_s, halo_r, wz_s, wz_r, wx_s, wx_r, wc_s, wc_r,
     rc_s, rc_r, rx_s, rx_r, rz_s, rz_r, ag_s, ag_r,
 ):
@@ -140,7 +140,12 @@
     fan_scale = 1.0 / math.sqrt(fan_size)
     band = lax.axis_index("space")
     mine = lax.axis_index("dp")
+    group = lax.axis_index("groups")
     core = band % 2
+    slot = 2 * group + core
+    slot_cross = 2 * (1 - group) + core
+    far_half = 1 - mine // 2
+    order = (3 * far_half, 1 + far_half, 2 * (mine // 2) + 1 - mine % 2, mine)
     pair = band + 1 - 2 * core
     cross = (band + 2) % 4
 
@@ -160,7 +165,18 @@
             barrier, inc=1, device_id={"dp": (mine + j) % data_count}, device_id_type=MESH
         )
 
-    def unit_of(rows, gains):
+    pl.semaphore_signal(barrier, inc=1, device_id={"groups": 1 - group}, device_id_type=MESH)
+
+    loads = [
+        pltpu.make_async_copy(src, dst, load_s.at[n])
+        for n, (src, dst) in enumerate(
+            ((raw_hbm, raw_ref), (gain_hbm, gain_row), (x_hbm, x_ref), (cot_hbm, cot_ref))
+        )
+    ]
+    for one in loads:
+        one.start()
+
+    def unit_of(rows):
         row_mean = jnp.mean(rows, axis=1, keepdims=True)
         centred = rows - row_mean
         row_var = jnp.mean(centred * centred, axis=1, keepdims=True)
@@ -170,39 +186,47 @@
     def std_step(k, carry):
         rows = rows_at(k * piece_rows, piece_rows)
         gains = gain_ref[rows, :]
-        unit, _ = unit_of(raw_ref[rows, :], gains)
+        unit, _ = unit_of(raw_ref[rows, :])
         std[rows_at(mine * owner_rows + k * piece_rows, piece_rows), :] = (
             gains * unit * fan_scale
         ).astype(BF16)
         return carry
 
+    pl.semaphore_wait(barrier, 3 + data_count)
+
+    up = copy(cot_hbm.at[pl.ds(0, cols), :], halo.at[1], halo_s.at[0], halo_r.at[1],
+              {"space": (band + 3) % 4})
+    down = copy(cot_hbm.at[pl.ds(pixels - cols, cols), :], halo.at[0], halo_s.at[1], halo_r.at[0],
+                {"space": (band + 1) % 4})
+
+    @pl.when(band > 0)
+    def _():
+        up.start()
+
+    @pl.when(band < 3)
+    def _():
+        down.start()
+
+    loads[0].wait()
+    loads[1].wait()
+    diagonal = lax.broadcasted_iota(jnp.int32, (owner_rows, owner_rows), 0) == (
+        lax.broadcasted_iota(jnp.int32, (owner_rows, owner_rows), 1)
+    )
+    gain_ref[...] = jnp.sum(jnp.where(diagonal, gain_row[...], 0.0), axis=1, keepdims=True)
+
     lax.fori_loop(0, 4, std_step, 0)
-
-    pl.semaphore_wait(barrier, 2 + data_count)
-
-    up = copy(cot_ref.at[pl.ds(0, cols), :], halo.at[1], halo_s.at[0], halo_r.at[1],
-              {"space": (band + 3) % 4})
-    down = copy(cot_ref.at[pl.ds(pixels - cols, cols), :], halo.at[0], halo_s.at[1], halo_r.at[0],
-                {"space": (band + 1) % 4})
-
-    @pl.when(band > 0)
-    def _():
-        up.start()
-
-    @pl.when(band < 3)
-    def _():
-        down.start()
 
     def std_piece(owner, quarter):
         return std.at[rows_at(owner * owner_rows + quarter * piece_rows, piece_rows), :]
 
     wz = []
-    for j in range(1, data_count):
-        own = std_piece(mine, band)
-        wz.append(copy(own, own, wz_s.at[j - 1], wz_r.at[j - 1],
-                       {"dp": (mine + j) % data_count}))
+    own = std_piece(mine, slot)
+    for t in range(3):
+        wz.append(copy(own, own, wz_s.at[t], wz_r.at[mine], {"dp": order[t]}))
         wz[-1].start()
 
+    loads[2].wait()
+    loads[3].wait()
     gpad[pl.ds(cols, pixels), :] = (alpha_skip * cot_ref[...].astype(F32)).astype(BF16)
 
     row_id = lax.broadcasted_iota(jnp.int32, (pixels, width), 0) % cols
@@ -252,60 +276,55 @@
     def place(owner, quarter):
         return rows_at(owner * owner_rows + quarter * piece_rows, piece_rows)
 
-    halves = 2 if data_count % 2 == 0 and group_count % 2 == 0 else 1
-    rc = {}
-    for half in range(halves):
-        lax.fori_loop(
-            half * group_count // halves, (half + 1) * group_count // halves, weight_step, 0
-        )
-        for d in range(half * data_count // halves, (half + 1) * data_count // halves):
+    half_groups = group_count // 2
+    rc = []
+    for half in range(2):
+        first = half_groups * (far_half if half == 0 else 1 - far_half)
+        lax.fori_loop(0, half_groups, lambda k, c: weight_step(first + k, c), 0)
+        for d in range(2 * half, 2 * half + 2):
             for t in range(2):
-                at = place(d, 1 - core + 2 * t)
+                at = place(order[d], 1 - core + 2 * t)
                 sendb[at, :] = part[at, :].astype(BF16)
                 n = 2 * d + t
-                rc[n] = copy(sendb.at[at, :], got_core.at[n], rc_s.at[n], rc_r.at[n],
-                             {"space": pair})
-                rc[n].start()
+                rc.append(copy(sendb.at[at, :], got_core.at[n], rc_s.at[n], rc_r.at[n],
+                               {"space": pair}))
+                rc[-1].start()
 
     rx = []
-    for d in range(data_count):
+    for d in range(4):
         for t in range(2):
-            n = 2 * d + t
-            rc[n].wait_recv()
-        other = cross // 2
-        at = place(d, cross)
-        sendb[at, :] = (part[at, :] + got_core[2 * d + other].astype(F32)).astype(BF16)
+            rc[2 * d + t].wait_recv()
+        at = place(order[d], cross)
+        sendb[at, :] = (part[at, :] + got_core[2 * d + cross // 2].astype(F32)).astype(BF16)
         rx.append(copy(sendb.at[at, :], got_x.at[d], rx_s.at[d], rx_r.at[d], {"space": cross}))
         rx[-1].start()
 
     wx = []
-    for j in range(1, data_count):
-        wz[j - 1].wait_recv()
-        piece = std_piece((mine + data_count - j) % data_count, band)
-        wx.append(copy(piece, piece, wx_s.at[j - 1], wx_r.at[j - 1], {"space": cross}))
+    for t in (2, 1, 0):
+        piece = std_piece(order[t], slot)
+        copy(piece, piece, wz_s.at[t], wz_r.at[order[t]], {"dp": order[t]}).wait_recv()
+        wx.append(copy(piece, piece, wx_s.at[t], wx_r.at[t], {"groups": 1 - group}))
         wx[-1].start()
 
-    for d in range(data_count):
+    rz = []
+    for d in range(4):
         rx[d].wait_recv()
-        at = place(d, band)
+        at = place(order[d], band)
         total = part[at, :] + got_core[2 * d + band // 2].astype(F32) + got_x[d].astype(F32)
-        part[at, :] = total
-        sendb[at, :] = total.astype(BF16)
-    rz = []
-    for j in range(1, data_count):
-        owner = (mine + j) % data_count
-        rz.append(copy(sendb.at[place(owner, band), :], got_z.at[j - 1], rz_s.at[j - 1],
-                       rz_r.at[j - 1], {"dp": owner}))
-        rz[-1].start()
+        if d == 3:
+            part[at, :] = total
+        else:
+            sendb[at, :] = total.astype(BF16)
+            rz.append(copy(sendb.at[at, :], got_z.at[mine], rz_s.at[d], rz_r.at[mine],
+                           {"dp": order[d]}))
+            rz[-1].start()
 
     wc = []
-    for j in range(1, data_count):
-        wx[j - 1].wait_recv()
-        owner = (mine + data_count - j) % data_count
-        for t, quarter in enumerate((band, cross)):
-            n = 2 * (j - 1) + t
-            piece = std_piece(owner, quarter)
-            wc.append(copy(piece, piece, wc_s.at[n], wc_r.at[n], {"space": pair}))
+    for n, t in enumerate((2, 1, 0)):
+        wx[n].wait_recv()
+        for e, quarter in enumerate((slot, slot_cross)):
+            piece = std_piece(order[t], quarter)
+            wc.append(copy(piece, piece, wc_s.at[2 * t + e], wc_r.at[2 * t + e], {"space": pair}))
             wc[-1].start()
     for one in wc:
         one.wait_recv()
@@ -324,16 +343,25 @@
         grad_ref[:, at] = grad.astype(BF16)
         return carry
 
-    lax.fori_loop(0, group_count // 2, back_step, 0)
+    lax.fori_loop(0, half_groups, back_step, 0)
+    outs = []
+    half_cols = chan_count // 2
+
+    def write(src, dst):
+        outs.append(pltpu.make_async_copy(src, dst, out_s.at[len(outs)]))
+        outs[-1].start()
+
+    write(grad_ref.at[:, pl.ds(0, half_cols)], grad_hbm.at[:, pl.ds(0, half_cols)])
 
     total = part[place(mine, band), :]
-    for j in range(1, data_count):
-        rz[j - 1].wait_recv()
-        total = total + got_z[j - 1].astype(F32)
+    for t in (2, 1, 0):
+        here = sendb.at[place(order[t], band), :]
+        copy(here, got_z.at[order[t]], rz_s.at[t], rz_r.at[order[t]], {"dp": order[t]}).wait_recv()
+        total = total + got_z[order[t]].astype(F32)
     grad_standard = total * (1.0 / total_images)
     rows = rows_at(band * piece_rows, piece_rows)
     gains = gain_ref[rows, :]
-    unit, inv_std = unit_of(raw_ref[rows, :], gains)
+    unit, inv_std = unit_of(raw_ref[rows, :])
     grad_gain = jnp.sum(grad_standard * unit, axis=1, keepdims=True) * fan_scale
     grad_unit = grad_standard * gains * fan_scale
     centre_term = jnp.mean(grad_unit, axis=1, keepdims=True)
@@ -345,15 +373,28 @@
     gathered[band, :, pl.ds(0, fan_size)] = grad_raw.astype(BF16)
     gathered[band, :, pl.ds(fan_size, 128)] = jnp.where(lane == 0, high, low).astype(BF16)
     ag = []
-    for j in range(1, 4):
-        ag.append(copy(gathered.at[band], gathered.at[band], ag_s.at[j - 1], ag_r.at[j - 1],
-                       {"space": (band + j) % 4}))
+    for n, (quarter, to) in enumerate(((band, cross), (band, pair), (cross, pair))):
+        if n == 2:
+            lax.fori_loop(half_groups, group_count - 1, back_step, 0)
+            ag[0].wait_recv()
+        block = gathered.at[quarter]
+        ag.append(copy(block, block, ag_s.at[n], ag_r.at[n], {"space": to}))
         ag[-1].start()
-    lax.fori_loop(group_count // 2, group_count, back_step, 0)
-    for one in ag:
-        one.wait_recv()
+    lax.fori_loop(group_count - 1, group_count, back_step, 0)
+    write(grad_ref.at[:, pl.ds(half_cols, half_cols)], grad_hbm.at[:, pl.ds(half_cols, half_cols)])
+    ag[1].wait_recv()
+    ag[2].wait_recv()
+    lane_id = lax.broadcasted_iota(jnp.int32, (piece_rows, owner_rows), 1)
+    line_id = lax.broadcasted_iota(jnp.int32, (piece_rows, owner_rows), 0)
+    gain_line = jnp.zeros((1, owner_rows), F32)
     for q in range(4):
-        ws_ref[pl.ds(q * piece_rows, piece_rows), :] = gathered[q]
+        write(gathered.at[q, :, pl.ds(0, fan_size)], ws_hbm.at[pl.ds(q * piece_rows, piece_rows), :])
+        both = gathered[q, :, pl.ds(fan_size, 128)].astype(F32)
+        column = both[:, 0:1] + both[:, 1:2]
+        gain_line = gain_line + jnp.sum(
+            jnp.where(lane_id == line_id + q * piece_rows, column, 0.0), axis=0, keepdims=True
+        )
+    gains_ref[...] = gain_line
 
     @pl.when(band > 0)
     def _():
@@ -363,8 +404,30 @@
     def _():
         down.wait_send()
 
-    for one in wz + list(rc.values()) + rx + wx + rz + wc + ag:
+    for one in outs:
+        one.wait()
+    for one in wz + rc + rx + wx + rz + wc + ag:
         one.wait_send()
+
+
+def widen_kernel(grad_ref, rounded_ref, gains_ref, grad_out, raw_out, gains_out, narrow, wide, sems):
+    load = pltpu.make_async_copy(rounded_ref, narrow, sems.at[6])
+    load.start()
+    copies = [
+        pltpu.make_async_copy(grad_ref, grad_out, sems.at[0]),
+        pltpu.make_async_copy(gains_ref, gains_out, sems.at[1]),
+    ]
+    for one in copies:
+        one.start()
+    load.wait()
+    rows = narrow.shape[0] // 4
+    for k in range(4):
+        at = pl.ds(k * rows, rows)
+        wide[at, :] = narrow[at, :].astype(F32)
+        copies.append(pltpu.make_async_copy(wide.at[at, :], raw_out.at[at, :], sems.at[2 + k]))
+        copies[-1].start()
+    for one in copies:
+        one.wait()
 
 
 def local_kernel(inputs, cotangent, kernel_raw, kernel_gain):
@@ -377,15 +440,24 @@
     dma = pltpu.SemaphoreType.DMA
     peers = data_count - 1
     vmem = pl.BlockSpec(memory_space=pltpu.VMEM)
-    grad, packed = pl.pallas_call(
+    hbm = pl.BlockSpec(memory_space=pltpu.HBM)
+    grad, rounded, gains = pl.pallas_call(
         functools.partial(block_kernel, images * data_count, data_count),
         out_shape=(
             jax.ShapeDtypeStruct((pixels, chan_count), BF16),
-            jax.ShapeDtypeStruct((owner_rows, fan_size + 128), BF16),
+            jax.ShapeDtypeStruct((owner_rows, fan_size), BF16),
+            jax.ShapeDtypeStruct((1, owner_rows), F32),
         ),
-        in_specs=[vmem] * 4,
-        out_specs=(vmem, vmem),
+        in_specs=[hbm] * 4,
+        out_specs=(hbm, hbm, vmem),
         scratch_shapes=[
+            pltpu.VMEM((pixels, chan_count), BF16),
+            pltpu.VMEM((pixels, chan_count), BF16),
+            pltpu.VMEM((owner_rows, fan_size), F32),
+            pltpu.VMEM((1, owner_rows), F32),
+            pltpu.VMEM((owner_rows, 1), F32),
+            pltpu.VMEM((pixels, chan_count), BF16),
+            dma((4,)), dma((6,)),
             pltpu.VMEM((2, band_cols, chan_count), BF16),
             pltpu.VMEM((pixels + 2 * band_cols, chan_count), BF16),
             pltpu.VMEM((pixels, 3 * chan_count), BF16),
@@ -395,19 +467,19 @@
             pltpu.VMEM((chan_count, fan_size), BF16),
             pltpu.VMEM((2 * data_count, piece_rows, fan_size), BF16),
             pltpu.VMEM((data_count, piece_rows, fan_size), BF16),
-            pltpu.VMEM((peers, piece_rows, fan_size), BF16),
+            pltpu.VMEM((data_count, piece_rows, fan_size), BF16),
             pltpu.VMEM((4, piece_rows, fan_size + 128), BF16),
             dma((2,)), dma((2,)),
-            dma((peers,)), dma((peers,)),
+            dma((peers,)), dma((data_count,)),
             dma((peers,)), dma((peers,)),
             dma((2 * peers,)), dma((2 * peers,)),
             dma((2 * data_count,)), dma((2 * data_count,)),
             dma((data_count,)), dma((data_count,)),
-            dma((peers,)), dma((peers,)),
+            dma((peers,)), dma((data_count,)),
             dma((3,)), dma((3,)),
         ],
         compiler_params=pltpu.CompilerParams(
-            collective_id=0, has_side_effects=True, vmem_limit_bytes=48 * 1024 * 1024
+            collective_id=0, has_side_effects=True, vmem_limit_bytes=60 * 1024 * 1024
         ),
         cost_estimate=pl.CostEstimate(
             flops=4 * pixels * chan_count * fan_size,
@@ -418,11 +490,24 @@
         inputs.reshape(pixels, chan_count),
         cotangent.reshape(pixels, chan_count),
         kernel_raw,
-        kernel_gain[:, None],
+        kernel_gain.reshape(1, owner_rows),
     )
-    grad_raw = packed[:, :fan_size].astype(F32)
-    grad_gain = packed[:, fan_size].astype(F32) + packed[:, fan_size + 1].astype(F32)
-    return (grad.reshape(inputs.shape), grad_raw, grad_gain)
+    grad, grad_raw, grad_gain = pl.pallas_call(
+        widen_kernel,
+        out_shape=(
+            jax.ShapeDtypeStruct((pixels, chan_count), BF16),
+            jax.ShapeDtypeStruct((owner_rows, fan_size), F32),
+            jax.ShapeDtypeStruct((1, owner_rows), F32),
+        ),
+        in_specs=[hbm] * 3,
+        out_specs=(hbm, hbm, hbm),
+        scratch_shapes=[
+            pltpu.VMEM((owner_rows, fan_size), BF16),
+            pltpu.VMEM((owner_rows, fan_size), F32),
+            dma((7,)),
+        ],
+    )(grad, rounded, gains)
+    return (grad.reshape(inputs.shape), grad_raw, grad_gain.reshape(owner_rows))
 
 
 def solution(mesh):
@@ -440,6 +525,8 @@
         replicas = mesh.shape["groups"] * data_count
         fits = (
             mesh.shape["space"] == 4
+            and data_count == 4
+            and mesh.shape["groups"] == 2
             and images == replicas
             and chan_count % (64 * data_count) == 0
             and (chan_count // (fan_size // 9)) % 2 == 0

time: 47.7 us -> 48.8 us (1.023)
  Pallas kernels: 40.4 us -> 48 us
  local copies, waits for them, and re-layouts: 4.69 us -> 0 us
  other arithmetic: 1.72 us -> 0 us
    pallas_call x0 -> x1, Pallas kernels: none -> 13.1 us  [local_kernel(): pl.pallas_call(widen_kernel, out_shape=(jax.ShapeDtypeStruct((pixels, cha...]
    pallas_call x1, Pallas kernels: 40.4 us -> 34.8 us  [local_kernel(): pl.pallas_call(functools.partial(block_kernel, images * data_count, data_...]
    unnamed x9 -> x0, local copies, waits for them, and re-layouts: 4.57 us -> none
    convert_element_type x1 -> x0, other arithmetic: 0.97 us -> none  [local_kernel(): grad_raw = packed[:, :fan_size].astype(F32)]
    add x1 -> x0, other arithmetic: 0.75 us -> none  [local_kernel(): packed[:, fan_size].astype(F32) + packed[:, fan_size + 1].astype(F32)]
where the time goes in v2:
time: 48.8 us; the launch traced here: 48.6 us
  Pallas kernels  48 us (98%)
  between operations  0.64 us (1%)
    pallas_call x1, Pallas kernels, local_kernel(): pl.pallas_call(functools.partial(block_kernel, images * data_count, data_...  34.8 us
    pallas_call x1, Pallas kernels, local_kernel(): pl.pallas_call(widen_kernel, out_shape=(jax.ShapeDtypeStruct((pixels, cha...  13.1 us

profile of v2, /device:TPU:1, one launch (start us, length us, event | category | flops | bytes accessed | tf_op | source)
XLA Modules:
  0.0 48.6 jit_solution(9029600312926489479)
XLA Ops:
  0.6 34.8 %shard_map.67 = (bf16[256,768]{1,0:T(8,128)(2,1)}, bf16[192,1152]{1,0:T(8,128)(2,1)}, f32[1,192]{1,0:T(1,128)}) custom-call(bf16[256,768]{1,0:T(8,128)(2,1)} %bitcast.5, bf16[256,768]{1,0:T(8,128)(2,1)} %bitcast.6, f32[192,1152]{1,0:T(8,128)} %raw_hbm.1, f32[1,192]{1,0:T(1,128)} %bitcast.8), custom_call_target="tpu_custom_call" | custom-call | flops 905969664 | bytes 1572864 | tf_op jit(solution)/shard_map/pallas_call | solution.py:444
  35.5 13.1 %shard_map.68 = (bf16[256,768]{1,0:T(8,128)(2,1)}, f32[192,1152]{1,0:T(8,128)}, f32[1,192]{1,0:T(1,128)}) custom-call(bf16[256,768]{1,0:T(8,128)(2,1)} %get-tuple-element.9.grad_ref, bf16[192,1152]{1,0:T(8,128)(2,1)} %get-tuple-element.10.rounded_ref, f32[1,192]{1,0:T(1,128)} %get-tuple-element.11.gains_ref), custom_call_target="tpu_custom_call" | custom-call | tf_op jit(solution)/shard_map/pallas_call | solution.py:495

commit v3 on v2

--- a/solution.py
+++ b/solution.py
@@ -410,24 +410,39 @@
         one.wait_send()
 
 
-def widen_kernel(grad_ref, rounded_ref, gains_ref, grad_out, raw_out, gains_out, narrow, wide, sems):
-    load = pltpu.make_async_copy(rounded_ref, narrow, sems.at[6])
-    load.start()
-    copies = [
-        pltpu.make_async_copy(grad_ref, grad_out, sems.at[0]),
-        pltpu.make_async_copy(gains_ref, gains_out, sems.at[1]),
-    ]
-    for one in copies:
-        one.start()
-    load.wait()
-    rows = narrow.shape[0] // 4
-    for k in range(4):
+def widen_kernel(
+    grad_ref, rounded_ref, gains_ref, grad_out, raw_out, gains_out, held, narrow, wide, line, sems
+):
+    halves = []
+    middle = grad_ref.shape[0] // 2
+    for k in range(2):
+        at = pl.ds(k * middle, middle)
+        halves.append((
+            pltpu.make_async_copy(grad_ref.at[at, :], held.at[at, :], sems.at[k]),
+            pltpu.make_async_copy(held.at[at, :], grad_out.at[at, :], sems.at[2 + k]),
+        ))
+    rows = narrow.shape[0] // 2
+    for k in range(2):
         at = pl.ds(k * rows, rows)
-        wide[at, :] = narrow[at, :].astype(F32)
-        copies.append(pltpu.make_async_copy(wide.at[at, :], raw_out.at[at, :], sems.at[2 + k]))
-        copies[-1].start()
-    for one in copies:
-        one.wait()
+        halves.append((
+            pltpu.make_async_copy(rounded_ref.at[at, :], narrow.at[at, :], sems.at[4 + k]),
+            pltpu.make_async_copy(wide.at[at, :], raw_out.at[at, :], sems.at[6 + k]),
+        ))
+    halves.append((
+        pltpu.make_async_copy(gains_ref, line, sems.at[8]),
+        pltpu.make_async_copy(line, gains_out, sems.at[9]),
+    ))
+    order = (2, 3, 0, 1, 4)
+    for n in order:
+        halves[n][0].start()
+    for n in order:
+        halves[n][0].wait()
+        if n in (2, 3):
+            at = pl.ds((n - 2) * rows, rows)
+            wide[at, :] = narrow[at, :].astype(F32)
+        halves[n][1].start()
+    for n in order:
+        halves[n][1].wait()
 
 
 def local_kernel(inputs, cotangent, kernel_raw, kernel_gain):
@@ -502,10 +517,13 @@
         in_specs=[hbm] * 3,
         out_specs=(hbm, hbm, hbm),
         scratch_shapes=[
+            pltpu.VMEM((pixels, chan_count), BF16),
             pltpu.VMEM((owner_rows, fan_size), BF16),
             pltpu.VMEM((owner_rows, fan_size), F32),
-            dma((7,)),
+            pltpu.VMEM((1, owner_rows), F32),
+            dma((10,)),
         ],
+        compiler_params=pltpu.CompilerParams(vmem_limit_bytes=60 * 1024 * 1024),
     )(grad, rounded, gains)
     return (grad.reshape(inputs.shape), grad_raw, grad_gain.reshape(owner_rows))
 

time: 48.8 us -> 37.7 us (0.77)
  Pallas kernels: 48 us -> 36.9 us
    pallas_call x1, Pallas kernels: 13.1 us -> 2.09 us  [local_kernel(): pl.pallas_call(widen_kernel, out_shape=(jax.ShapeDtypeStruct((pixels, cha...]
where the time goes in v3:
time: 37.7 us; the launch traced here: 37.6 us
  Pallas kernels  36.9 us (98%)
  between operations  0.64 us (2%)
    pallas_call x1, Pallas kernels, local_kernel(): pl.pallas_call(functools.partial(block_kernel, images * data_count, data_...  34.8 us
    pallas_call x1, Pallas kernels, local_kernel(): pl.pallas_call(widen_kernel, out_shape=(jax.ShapeDtypeStruct((pixels, cha...  2.09 us

profile of v3, /device:TPU:1, one launch (start us, length us, event | category | flops | bytes accessed | tf_op | source)
XLA Modules:
  0.0 37.6 jit_solution(2509877962827755208)
XLA Ops:
  0.6 34.8 %shard_map.67 = (bf16[256,768]{1,0:T(8,128)(2,1)}, bf16[192,1152]{1,0:T(8,128)(2,1)}, f32[1,192]{1,0:T(1,128)}) custom-call(bf16[256,768]{1,0:T(8,128)(2,1)} %bitcast.5, bf16[256,768]{1,0:T(8,128)(2,1)} %bitcast.6, f32[192,1152]{1,0:T(8,128)} %raw_hbm.1, f32[1,192]{1,0:T(1,128)} %bitcast.8), custom_call_target="tpu_custom_call" | custom-call | flops 905969664 | bytes 1572864 | tf_op jit(solution)/shard_map/pallas_call | solution.py:459
  35.5 2.1 %shard_map.68 = (bf16[256,768]{1,0:T(8,128)(2,1)}, f32[192,1152]{1,0:T(8,128)}, f32[1,192]{1,0:T(1,128)}) custom-call(bf16[256,768]{1,0:T(8,128)(2,1)} %get-tuple-element.9.grad_ref, bf16[192,1152]{1,0:T(8,128)(2,1)} %get-tuple-element.10.rounded_ref, f32[1,192]{1,0:T(1,128)} %get-tuple-element.11.gains_ref), custom_call_target="tpu_custom_call" | custom-call | tf_op jit(solution)/shard_map/pallas_call | solution.py:510

commit v4 on v3

--- a/solution.py
+++ b/solution.py
@@ -221,7 +221,7 @@
 
     wz = []
     own = std_piece(mine, slot)
-    for t in range(3):
+    for t in (2, 1, 0):
         wz.append(copy(own, own, wz_s.at[t], wz_r.at[mine], {"dp": order[t]}))
         wz[-1].start()
 
@@ -245,6 +245,21 @@
 
     lax.fori_loop(0, group_count, act_step, 0)
 
+    def taps(g, chosen):
+        at = pl.ds(pl.multiple_of(g * width, width), width)
+        right = hs[:, pl.ds(pl.multiple_of(g * wide, width), wide)]
+        for a in chosen:
+            left = gpad[pl.ds((2 - a) * cols, pixels), at]
+            part[at, pl.ds(a * wide, wide)] = lax.dot_general(
+                left, right, (((0,), (0,)), ((), ())), preferred_element_type=F32
+            )
+
+    def middle_step(g, carry):
+        taps(g, (1,))
+        return carry
+
+    lax.fori_loop(0, group_count, middle_step, 0)
+
     @pl.when(band > 0)
     def _():
         down.wait_recv()
@@ -264,19 +279,21 @@
         gpad[pl.ds(cols + pixels, cols), :] = jnp.zeros((cols, chan_count), BF16)
 
     def weight_step(g, carry):
-        at = pl.ds(pl.multiple_of(g * width, width), width)
-        right = hs[:, pl.ds(pl.multiple_of(g * wide, width), wide)]
-        for a in range(3):
-            left = gpad[pl.ds((2 - a) * cols, pixels), at]
-            part[pl.ds(pl.multiple_of(g * width, width), width), pl.ds(a * wide, wide)] = (
-                lax.dot_general(left, right, (((0,), (0,)), ((), ())), preferred_element_type=F32)
-            )
+        taps(g, (0, 2))
         return carry
 
     def place(owner, quarter):
         return rows_at(owner * owner_rows + quarter * piece_rows, piece_rows)
 
     half_groups = group_count // 2
+    wx = []
+
+    def forward(t):
+        piece = std_piece(order[t], slot)
+        copy(piece, piece, wz_s.at[t], wz_r.at[order[t]], {"dp": order[t]}).wait_recv()
+        wx.append(copy(piece, piece, wx_s.at[t], wx_r.at[t], {"groups": 1 - group}))
+        wx[-1].start()
+
     rc = []
     for half in range(2):
         first = half_groups * (far_half if half == 0 else 1 - far_half)
@@ -298,13 +315,18 @@
         sendb[at, :] = (part[at, :] + got_core[2 * d + cross // 2].astype(F32)).astype(BF16)
         rx.append(copy(sendb.at[at, :], got_x.at[d], rx_s.at[d], rx_r.at[d], {"space": cross}))
         rx[-1].start()
-
-    wx = []
-    for t in (2, 1, 0):
-        piece = std_piece(order[t], slot)
-        copy(piece, piece, wz_s.at[t], wz_r.at[order[t]], {"dp": order[t]}).wait_recv()
-        wx.append(copy(piece, piece, wx_s.at[t], wx_r.at[t], {"groups": 1 - group}))
-        wx[-1].start()
+        if d > 0:
+            forward(3 - d)
+
+    wc = []
+
+    def forward_pair(n):
+        t = 2 - n
+        wx[n].wait_recv()
+        for e, quarter in enumerate((slot, slot_cross)):
+            piece = std_piece(order[t], quarter)
+            wc.append(copy(piece, piece, wc_s.at[2 * t + e], wc_r.at[2 * t + e], {"space": pair}))
+            wc[-1].start()
 
     rz = []
     for d in range(4):
@@ -318,14 +340,9 @@
             rz.append(copy(sendb.at[at, :], got_z.at[mine], rz_s.at[d], rz_r.at[mine],
                            {"dp": order[d]}))
             rz[-1].start()
-
-    wc = []
-    for n, t in enumerate((2, 1, 0)):
-        wx[n].wait_recv()
-        for e, quarter in enumerate((slot, slot_cross)):
-            piece = std_piece(order[t], quarter)
-            wc.append(copy(piece, piece, wc_s.at[2 * t + e], wc_r.at[2 * t + e], {"space": pair}))
-            wc[-1].start()
+        if d > 0:
+            forward_pair(d - 1)
+
     for one in wc:
         one.wait_recv()
 

time: 37.7 us -> 36.6 us (0.971)
  Pallas kernels: 36.9 us -> 35.8 us
    pallas_call x1, Pallas kernels: 34.8 us -> 33.7 us  [local_kernel(): pl.pallas_call(functools.partial(block_kernel, images * data_count, data_...]
where the time goes in v4:
time: 36.6 us; the launch traced here: 36.4 us
  Pallas kernels  35.8 us (98%)
  between operations  0.64 us (2%)
    pallas_call x1, Pallas kernels, local_kernel(): pl.pallas_call(functools.partial(block_kernel, images * data_count, data_...  33.7 us
    pallas_call x1, Pallas kernels, local_kernel(): pl.pallas_call(widen_kernel, out_shape=(jax.ShapeDtypeStruct((pixels, cha...  2.09 us

profile of v4, /device:TPU:1, one launch (start us, length us, event | category | flops | bytes accessed | tf_op | source)
XLA Modules:
  0.0 36.4 jit_solution(10515039353103087584)
XLA Ops:
  0.6 33.7 %shard_map.67 = (bf16[256,768]{1,0:T(8,128)(2,1)}, bf16[192,1152]{1,0:T(8,128)(2,1)}, f32[1,192]{1,0:T(1,128)}) custom-call(bf16[256,768]{1,0:T(8,128)(2,1)} %bitcast.5, bf16[256,768]{1,0:T(8,128)(2,1)} %bitcast.6, f32[192,1152]{1,0:T(8,128)} %raw_hbm.1, f32[1,192]{1,0:T(1,128)} %bitcast.8), custom_call_target="tpu_custom_call" | custom-call | flops 905969664 | bytes 1572864 | tf_op jit(solution)/shard_map/pallas_call | solution.py:476
  34.3 2.1 %shard_map.68 = (bf16[256,768]{1,0:T(8,128)(2,1)}, f32[192,1152]{1,0:T(8,128)}, f32[1,192]{1,0:T(1,128)}) custom-call(bf16[256,768]{1,0:T(8,128)(2,1)} %get-tuple-element.9.grad_ref, bf16[192,1152]{1,0:T(8,128)(2,1)} %get-tuple-element.10.rounded_ref, f32[1,192]{1,0:T(1,128)} %get-tuple-element.11.gains_ref), custom_call_target="tpu_custom_call" | custom-call | tf_op jit(solution)/shard_map/pallas_call | solution.py:527

commit v5 on v4

--- a/solution.py
+++ b/solution.py
@@ -294,25 +294,24 @@
         wx.append(copy(piece, piece, wx_s.at[t], wx_r.at[t], {"groups": 1 - group}))
         wx[-1].start()
 
-    rc = []
+    rc = {}
     for half in range(2):
         first = half_groups * (far_half if half == 0 else 1 - far_half)
         lax.fori_loop(0, half_groups, lambda k, c: weight_step(first + k, c), 0)
-        for d in range(2 * half, 2 * half + 2):
-            for t in range(2):
-                at = place(order[d], 1 - core + 2 * t)
+        for t, line in enumerate((cross // 2, band // 2)):
+            for d in range(2 * half, 2 * half + 2):
+                at = place(order[d], 1 - core + 2 * line)
                 sendb[at, :] = part[at, :].astype(BF16)
                 n = 2 * d + t
-                rc.append(copy(sendb.at[at, :], got_core.at[n], rc_s.at[n], rc_r.at[n],
-                               {"space": pair}))
-                rc[-1].start()
+                rc[n] = copy(sendb.at[at, :], got_core.at[n], rc_s.at[n], rc_r.at[n],
+                             {"space": pair})
+                rc[n].start()
 
     rx = []
     for d in range(4):
-        for t in range(2):
-            rc[2 * d + t].wait_recv()
+        rc[2 * d].wait_recv()
         at = place(order[d], cross)
-        sendb[at, :] = (part[at, :] + got_core[2 * d + cross // 2].astype(F32)).astype(BF16)
+        sendb[at, :] = (part[at, :] + got_core[2 * d].astype(F32)).astype(BF16)
         rx.append(copy(sendb.at[at, :], got_x.at[d], rx_s.at[d], rx_r.at[d], {"space": cross}))
         rx[-1].start()
         if d > 0:
@@ -330,9 +329,10 @@
 
     rz = []
     for d in range(4):
+        rc[2 * d + 1].wait_recv()
         rx[d].wait_recv()
         at = place(order[d], band)
-        total = part[at, :] + got_core[2 * d + band // 2].astype(F32) + got_x[d].astype(F32)
+        total = part[at, :] + got_core[2 * d + 1].astype(F32) + got_x[d].astype(F32)
         if d == 3:
             part[at, :] = total
         else:
@@ -423,7 +423,7 @@
 
     for one in outs:
         one.wait()
-    for one in wz + rc + rx + wx + rz + wc + ag:
+    for one in wz + list(rc.values()) + rx + wx + rz + wc + ag:
         one.wait_send()
 
 

time: 36.6 us -> 36.5 us (level)
  no operation moved by 1% of the time
where the time goes in v5:
time: 36.5 us; the launch traced here: 36.4 us
  Pallas kernels  35.7 us (98%)
  between operations  0.64 us (2%)
    pallas_call x1, Pallas kernels, local_kernel(): pl.pallas_call(functools.partial(block_kernel, images * data_count, data_...  33.7 us
    pallas_call x1, Pallas kernels, local_kernel(): pl.pallas_call(widen_kernel, out_shape=(jax.ShapeDtypeStruct((pixels, cha...  2.09 us

profile of v5, /device:TPU:1, one launch (start us, length us, event | category | flops | bytes accessed | tf_op | source)
XLA Modules:
  0.0 36.4 jit_solution(8247439448490874168)
XLA Ops:
  0.6 33.7 %shard_map.67 = (bf16[256,768]{1,0:T(8,128)(2,1)}, bf16[192,1152]{1,0:T(8,128)(2,1)}, f32[1,192]{1,0:T(1,128)}) custom-call(bf16[256,768]{1,0:T(8,128)(2,1)} %bitcast.5, bf16[256,768]{1,0:T(8,128)(2,1)} %bitcast.6, f32[192,1152]{1,0:T(8,128)} %raw_hbm.1, f32[1,192]{1,0:T(1,128)} %bitcast.8), custom_call_target="tpu_custom_call" | custom-call | flops 905969664 | bytes 1572864 | tf_op jit(solution)/shard_map/pallas_call | solution.py:476
  34.3 2.1 %shard_map.68 = (bf16[256,768]{1,0:T(8,128)(2,1)}, f32[192,1152]{1,0:T(8,128)}, f32[1,192]{1,0:T(1,128)}) custom-call(bf16[256,768]{1,0:T(8,128)(2,1)} %get-tuple-element.9.grad_ref, bf16[192,1152]{1,0:T(8,128)(2,1)} %get-tuple-element.10.rounded_ref, f32[1,192]{1,0:T(1,128)} %get-tuple-element.11.gains_ref), custom_call_target="tpu_custom_call" | custom-call | tf_op jit(solution)/shard_map/pallas_call | solution.py:527
